TPU v7x, 32 devices: a whole 2x2x4 slice. The times are simulated.
32 devices in a mesh: grp: 2 (over x), freq: 8 (over z, y), rcv: 2 (over core).
Axes of the slice: x: 2, y: 2, z: 4, core: 2. Of those that a mesh axis runs over, the one named last changes fastest.
Arguments:
- kernel: bfloat16 [8, 2, 2048, 2048], P('freq', None, None, 'rcv'), may hold values from -0.09375 to 0.09375
- focus: bfloat16 [2048, 256, 256], P(('rcv', 'freq'), 'grp'), parts along dimension 1, may hold values from -6 to 6
- onset: int32 [2048, 256], P(None, 'grp'), parts along dimension 1, may hold values from 16 to 127
Outputs:
- updated: bfloat16 [2048, 256, 256], P(('rcv', 'freq'), 'grp'), parts along dimension 1
There are 2 independent parts, one for each index of `grp`. A program takes and returns all parts, laid end to end along the dimension named above; an argument that names none is the same for every part. Nothing has to cross between parts.
Inputs may be any that keep to these rules, and one draw needn't show every extreme that they name: onset is the direct-arrival time of focal point p at surface point x, in samples.
All inputs are finite; a program needn't handle non-finite values.
Results may differ from a plain program's by a relative error of at most 0.0028.
Values may be sent and summed in bfloat16 or wider, within the bound.
A program may use at most 128 MiB of HBM per device.

v0:
```python
import math

import jax
import jax.numpy as jnp
from jax import lax
from jax.sharding import PartitionSpec as P

F_DEV = 1


def tables(nt, nf):
    sample_count = jnp.arange(nt, dtype=jnp.int32)
    bins = jnp.arange(nf, dtype=jnp.int32) + 1
    phase = (bins[:, None] * sample_count[None, :] % nt).astype(jnp.float32) * (2.0 * math.pi / nt)
    forward = jnp.stack([jnp.cos(phase), -jnp.sin(phase)], axis=1)
    return (forward, forward * (2.0 / nt))


def taper_window(onset_rows, nt):
    sample_count = jnp.arange(nt, dtype=jnp.int32)
    edge = onset_rows[:, :, None]
    keep = (sample_count[None, None, :] < edge) | (sample_count[None, None, :] > nt - edge)
    return jnp.where(keep, 1.0, 0.0).astype(jnp.float32)


def slab_product(left_operand, right_operand):
    return jnp.einsum(
        "clj,cjw->clw", left_operand, right_operand, preferred_element_type=jnp.float32
    )


def slab_adjoint(left_operand, right_operand):
    return jnp.einsum(
        "lku,lki->lui", left_operand, right_operand, preferred_element_type=jnp.float32
    )


def shards(kernel, focus, onset):
    highest = lax.Precision.HIGHEST
    nfreq = lax.axis_size("freq")
    nt = focus.shape[2]
    forward, inverse = tables(nt, F_DEV * nfreq)
    rows = focus.shape[0]
    own_start = (lax.axis_index("rcv") * nfreq + lax.axis_index("freq")) * rows
    own_mask = taper_window(lax.dynamic_slice_in_dim(onset, own_start, rows, 0), nt)
    spec = jnp.einsum(
        "xpt,fct->fcxp", focus.astype(jnp.float32), forward, precision=highest
    ).astype(jnp.bfloat16)
    spec = lax.all_to_all(spec, "freq", split_axis=0, concat_axis=2, tiled=True)
    real_kernel = kernel[:, 0]
    imag_kernel = kernel[:, 1]
    real_part = slab_product(real_kernel, spec[:, 0]) - slab_product(imag_kernel, spec[:, 1])
    imag_part = slab_product(real_kernel, spec[:, 1]) + slab_product(imag_kernel, spec[:, 0])
    partial_value = jnp.stack([real_part, imag_part], axis=1)
    summed = lax.psum_scatter(partial_value, "rcv", scatter_dimension=2, tiled=True).astype(
        jnp.bfloat16
    )
    block = summed.shape[2] // nfreq
    start_time = (lax.axis_index("rcv") * nfreq + lax.axis_index("freq")) * block
    timed = lax.all_to_all(summed, "freq", split_axis=2, concat_axis=0, tiled=True)
    temporal_mask = taper_window(lax.dynamic_slice_in_dim(onset, start_time, block, 0), nt)
    minus = (
        jnp.einsum("fcxp,fct->xpt", timed.astype(jnp.float32), inverse, precision=highest)
        * temporal_mask
    )
    mspec = jnp.einsum("xpt,fct->fcxp", minus, forward, precision=highest).astype(jnp.bfloat16)
    returned = lax.all_to_all(mspec, "freq", split_axis=0, concat_axis=2, tiled=True)
    returned = lax.all_gather(returned, "rcv", axis=2, tiled=True)
    real_back = slab_adjoint(real_kernel, returned[:, 0]) + slab_adjoint(
        imag_kernel, returned[:, 1]
    )
    imag_back = slab_adjoint(real_kernel, returned[:, 1]) - slab_adjoint(
        imag_kernel, returned[:, 0]
    )
    hspec = jnp.stack([real_back, imag_back], axis=1).astype(jnp.bfloat16)
    arrival_reached = lax.all_to_all(hspec, "freq", split_axis=2, concat_axis=0, tiled=True)
    update = (
        jnp.einsum("fcxp,fct->xpt", arrival_reached.astype(jnp.float32), inverse, precision=highest)
        * own_mask
    )
    return (focus.astype(jnp.float32) + update).astype(jnp.bfloat16)


def solution(mesh):
    in_specs = (P("freq", None, None, "rcv"), P(("rcv", "freq"), "grp", None), P(None, "grp"))
    out_specs = P(("rcv", "freq"), "grp", None)
    return jax.shard_map(shards, mesh=mesh, in_specs=in_specs, out_specs=out_specs, check_vma=False)
```

profile of v0, /device:TPU:0, one launch (start us, length us, event | category | flops | bytes accessed | tf_op | source)
XLA Modules:
  0.0 182.2 jit_solution(8320679864506697726)
XLA Ops:
  6.5 0.0 reduce-scatter.2.cloned.1.call-start
  6.5 0.0 copy-start
  6.5 0.1 fusion.93
  6.7 9.1 %fusion.50 = bf16[8,2,128,128]{3,0,2,1:T(8,128)(2,1)S(1)} fusion(bf16[128,128,256]{2,1,0:T(8,128)(2,1)} %param.4, f32[8,1,256]{2,0,1:T(8,128)S(1)} %get-tuple-element.8, f32[8,1,256]{2,0,1:T(8,128)S(1)} %get-tuple-element.7), kind=kOutput, calls=%fused_computation.45 | convolution fusion | flops 805572608 | bytes 8929280 | tf_op jit(solution)/shard_map/xpt,fct->fcxp/dot_general | solution.py:46
  15.7 0.1 copy.14
  15.8 21.6 %all_to_all.72 = bf16[8,2,128,128]{3,2,1,0:T(8,128)(2,1)S(1)} all-to-all(bf16[8,2,128,128]{3,2,1,0:T(8,128)(2,1)S(1)} %copy.14), channel_id=1, replica_groups=mesh['grp'=2,'freq'=8,'rcv'=2] {'freq'}, dimensions={0} | all-to-all | bytes 1048576 | tf_op jit(solution)/shard_map/all_to_all | solution.py:49
  37.5 0.0 copy-done
  37.5 1.5 fusion.18
  39.0 1.5 fusion.20
  40.6 1.5 fusion.47
  42.1 1.6 fusion.41
  43.7 1.6 pad_maximum_fusion
  45.2 0.0 reduce-scatter.2.cloned.1.call-update
  45.3 8.8 %reduce-scatter.2.cloned.1.call-done = f32[1,2,1024,128]{2,3,1,0:T(8,128)} async-done(((f32[1,2,2048,128]{2,3,1,0:T(8,128)}), f32[1,2,1024,128]{2,3,1,0:T(8,128)}) %reduce-scatter.2.cloned.1.call-update) | async-done | bytes 1048592 | tf_op jit(solution)/shard_map/reduce_scatter | solution.py:55
  54.0 1.3 convert_element_type.46
  55.3 1.1 copy.16
  56.4 5.8 %all-to-all-start.1 = ((bf16[1,2,1024,128]{3,1,0,2:T(2,128)(2,1)}), bf16[1,2,1024,128]{3,1,0,2:T(2,128)(2,1)S(1)}, u32[]{:S(2)}, u32[]{:S(2)}) async-start(bf16[1,2,1024,128]{3,1,0,2:T(2,128)(2,1)} %copy.16), calls=%async_computation.2 | async-start | bytes 1048576 | tf_op jit(solution)/shard_map/all_to_all | solution.py:60
  62.2 0.2 all-gather.2.cloned.1.call-start
  62.4 0.9 broadcast_subtract_fusion
  63.3 13.9 %all-to-all-done.1 = bf16[1,2,1024,128]{3,1,0,2:T(2,128)(2,1)S(1)} async-done(((bf16[1,2,1024,128]{3,1,0,2:T(2,128)(2,1)}), bf16[1,2,1024,128]{3,1,0,2:T(2,128)(2,1)S(1)}, u32[]{:S(2)}, u32[]{:S(2)}) %all-to-all-start.1) | async-done | bytes 524320 | tf_op jit(solution)/shard_map/all_to_all | solution.py:60
  77.1 6.7 %fusion.75 = f32[128,128,256,1]{2,1,3,0:T(8,128)S(1)} fusion(bf16[1,2,8,128,128]{4,1,3,2,0:T(2,128)(2,1)S(1)} %bitcast.125, f32[8,1,256]{2,0,1:T(8,128)S(1)} %get-tuple-element.8, f32[8,1,256]{2,0,1:T(8,128)S(1)} %get-tuple-element.7), kind=kOutput, calls=%fused_computation.57 | convolution fusion | flops 805314560 | bytes 17317888 | tf_op jit(solution)/shard_map/fcxp,fct->xpt/dot_general | solution.py:63
  83.9 16.7 %fusion.53 = bf16[8,2,128,128]{3,0,2,1:T(8,128)(2,1)S(1)} fusion(f32[128,128,256,1]{2,1,3,0:T(8,128)S(1)} %fusion.75, s32[128,128]{1,0:T(8,128)S(1)} %get-tuple-element.5, s32[128,128]{1,0:T(8,128)S(1)} %get-tuple-element.6, f32[8,1,256]{2,0,1:T(8,128)S(1)} %get-tuple-element.8, f32[8,1,256]{2,0,1:T(8,128)S(1)} %get-tuple-element.7), kind=kOutput, calls=%fused_computation.46 | convolution fusion | flops 826544128 | bytes 17448960 | tf_op jit(solution)/shard_map/xpt,fct->fcxp/dot_general | solution.py:66
  100.6 0.1 copy.19
  100.7 18.1 %all_to_all.73 = bf16[8,2,128,128]{3,2,1,0:T(8,128)(2,1)S(1)} all-to-all(bf16[8,2,128,128]{3,2,1,0:T(8,128)(2,1)S(1)} %copy.19), channel_id=1, replica_groups=mesh['grp'=2,'freq'=8,'rcv'=2] {'freq'}, dimensions={0} | all-to-all | bytes 1048576 | tf_op jit(solution)/shard_map/all_to_all | solution.py:67
  118.8 0.8 copy.20
  119.6 0.0 all-gather.2.cloned.1.call-update
  119.7 8.2 %all-gather.2.cloned.1.call-done = bf16[1,2,2048,128]{3,2,1,0:T(8,128)(2,1)} async-done(((bf16[1,2,1024,128]{3,2,1,0:T(8,128)(2,1)}), bf16[1,2,2048,128]{3,2,1,0:T(8,128)(2,1)}) %all-gather.2.cloned.1.call-update) | async-done | bytes 1048592 | tf_op jit(solution)/shard_map/all_gather | solution.py:68
  127.9 0.0 copy-start.1
  127.9 3.2 %fusion.14 = f32[128,1024]{1,0:T(8,128)S(1)} fusion(bf16[1,2,2048,1024]{3,2,1,0:T(8,128)(2,1)} %param.3, bf16[1,2,2048,128]{3,2,1,0:T(8,128)(2,1)} %all-gather.2.cloned.1.call-done), kind=kOutput, calls=%fused_computation.16 | convolution fusion | flops 536870912 | bytes 5242880 | tf_op jit(solution)/shard_map/lku,lki->lui/dot_general | solution.py:33
  131.1 3.1 %fusion.16 = f32[128,1024]{1,0:T(8,128)S(1)} fusion(bf16[1,2,2048,1024]{3,2,1,0:T(8,128)(2,1)} %param.3, bf16[1,2,2048,128]{3,2,1,0:T(8,128)(2,1)} %all-gather.2.cloned.1.call-done), kind=kOutput, calls=%fused_computation.18 | convolution fusion | flops 536870912 | bytes 5242880 | tf_op jit(solution)/shard_map/lku,lki->lui/dot_general | solution.py:33
  134.2 0.0 copy-done.1
  134.2 3.0 %fusion.71 = bf16[1,1,1024,128]{2,3,1,0:T(8,128)(2,1)S(1)} fusion(f32[128,1024]{1,0:T(8,128)S(1)} %fusion.14, bf16[1,2,2048,1024]{3,2,1,0:T(8,128)(2,1)} %param.3, bf16[1,2,2048,128]{3,2,1,0:T(8,128)(2,1)S(1)} %copy-done.1), kind=kOutput, calls=%fused_computation.52 | convolution fusion | flops 537133056 | bytes 5505024 | tf_op jit(solution)/shard_map/lku,lki->lui/dot_general | solution.py:33
  137.2 2.9 %fusion.68 = bf16[1,1,1024,128]{2,3,1,0:T(8,128)(2,1)S(1)} fusion(f32[128,1024]{1,0:T(8,128)S(1)} %fusion.16, bf16[1,2,2048,1024]{3,2,1,0:T(8,128)(2,1)} %param.3, bf16[1,2,2048,128]{3,2,1,0:T(8,128)(2,1)S(1)} %copy-done.1), kind=kOutput, calls=%fused_computation.51 | convolution fusion | flops 537133056 | bytes 5505024 | tf_op jit(solution)/shard_map/lku,lki->lui/dot_general | solution.py:33
  140.1 0.1 pad_maximum_fusion.1
  140.2 0.4 copy.21
  140.6 20.5 %all_to_all.74 = bf16[1,2,1024,128]{3,1,0,2:T(2,128)(2,1)S(1)} all-to-all(bf16[1,2,1024,128]{3,1,0,2:T(2,128)(2,1)S(1)} %copy.21), channel_id=1, replica_groups=mesh['grp'=2,'freq'=8,'rcv'=2] {'freq'}, dimensions={2} | all-to-all | bytes 1048576 | tf_op jit(solution)/shard_map/all_to_all | solution.py:76
  161.1 14.3 %fusion.4 = bf16[128,128,256]{2,1,0:T(8,128)(2,1)} fusion(bf16[128,128,256]{2,1,0:T(8,128)(2,1)} %param.4, s32[128,128]{1,0:T(8,128)S(1)} %get-tuple-element.5, s32[128,128]{1,0:T(8,128)S(1)} %get-tuple-element.6, bf16[1,2,8,128,128]{4,1,3,2,0:T(2,128)(2,1)S(1)} %bitcast.131, f32[8,1,256]{2,0,1:T(8,128)S(1)} %get-tuple-element.8, ...), kind=kOutput, calls=%fused_computation.5 | convolution fusion | flops 838868992 | bytes 17448960 | tf_op jit(solution)/shard_map/fcxp,fct->xpt/dot_general | solution.py:78
  (2 shorter events, 0.0 us)
Async XLA Ops:
  6.5 47.5 %reduce-scatter.2.cloned.1.call-start = ((), (), s32[]{:S(2)}) async-start(), calls=%async_computation.5 | async-start | bytes 3145728 | tf_op jit(solution)/shard_map/reduce_scatter | solution.py:55
  6.5 31.0 %copy-start = (bf16[1,2,2048,1024]{3,2,1,0:T(8,128)(2,1)S(1)}, bf16[1,2,2048,1024]{3,2,1,0:T(8,128)(2,1)}, u32[]{:S(2)}) copy-start(bf16[1,2,2048,1024]{3,2,1,0:T(8,128)(2,1)} %param.3) | copy-start | bytes 25165828
  56.4 20.7 %all-to-all-start.1 = ((bf16[1,2,1024,128]{3,1,0,2:T(2,128)(2,1)}), bf16[1,2,1024,128]{3,1,0,2:T(2,128)(2,1)S(1)}, u32[]{:S(2)}, u32[]{:S(2)}) async-start(bf16[1,2,1024,128]{3,1,0,2:T(2,128)(2,1)} %copy.16), calls=%async_computation.2 | async-start | bytes 1048576 | tf_op jit(solution)/shard_map/all_to_all | solution.py:60
  62.2 65.7 %all-gather.2.cloned.1.call-start = ((), (), s32[]{:S(2)}) async-start(), calls=%async_computation.6 | async-start | bytes 1572864 | tf_op jit(solution)/shard_map/all_gather | solution.py:68
  127.9 6.3 %copy-start.1 = (bf16[1,2,2048,128]{3,2,1,0:T(8,128)(2,1)S(1)}, bf16[1,2,2048,128]{3,2,1,0:T(8,128)(2,1)}, u32[]{:S(2)}) copy-start(bf16[1,2,2048,128]{3,2,1,0:T(8,128)(2,1)} %all-gather.2.cloned.1.call-done) | copy-start | bytes 3145732
Sparse Core Ops, SparseCore 0:
  45.4 8.5 reduce-scatter.1
  119.8 8.0 all-gather.1
where the time goes:
time: 183 us; the launch traced here: 182 us
  matrix products  65.1 us (36%)
  blocking collectives  60.2 us (33%)
  waiting for transfers between devices  30.9 us (17%)
  between operations  13.6 us (7%)
  starting transfers between devices  5.99 us (3%)
  other arithmetic  3.89 us (2%)
  local copies, waits for them, and re-layouts  2.61 us (1%)
    all_to_all x1, blocking collectives, shards(): spec = lax.all_to_all(spec, 'freq', split_axis=0, concat_axis=2, tiled=True)  21.6 us
    all_to_all x1, blocking collectives, shards(): lax.all_to_all(hspec, 'freq', split_axis=2, concat_axis=0, tiled=True)  20.5 us
    all_to_all x1, blocking collectives, shards(): lax.all_to_all(mspec, 'freq', split_axis=0, concat_axis=2, tiled=True)  18.1 us
    dot_general x1, matrix products, shards(): jnp.einsum('xpt,fct->fcxp', minus, forward, precision=highest)  16.7 us
    dot_general x1, matrix products, shards(): jnp.einsum('fcxp,fct->xpt', arrival_reached.astype(jnp.float32), inverse,...  14.3 us
    all_to_all x1, waiting for transfers between devices, shards(): lax.all_to_all(summed, 'freq', split_axis=2, concat_axis=0, tiled=True)  13.9 us
    dot_general x4, matrix products, slab_adjoint(): jnp.einsum('lku,lki->lui', left_operand, right_operand, preferred_element...  12.2 us
    dot_general x1, matrix products, shards(): jnp.einsum('xpt,fct->fcxp', focus.astype(jnp.float32), forward, precision...  9.06 us
  transfers between devices with their start and end apart: 3, of which 3 were waited for; matrix products, arithmetic and copies ran while one was open for 0% of the time, Pallas kernels for 0%

commit v1 on v0

v1 whole, which is shorter than its diff:
```python
import functools
import math

import jax
import jax.numpy as jnp
import numpy as np
from jax import lax
from jax.experimental import pallas as pl
from jax.experimental.pallas import tpu as pltpu
from jax.sharding import PartitionSpec as P

MESH = pl.DeviceIdType.MESH
NSUB = 2
BF = jnp.bfloat16
F32 = jnp.float32


def forward_table(nt, nf):
    phase = ((np.arange(1, nf + 1)[:, None] * np.arange(nt)[None, :]) % nt) * (2.0 * math.pi / nt)
    return np.stack([np.cos(phase), -np.sin(phase)], axis=1).reshape(2 * nf, nt).astype(np.float32)


def split(table):
    high = table.astype(jnp.bfloat16)
    low = (table - high.astype(np.float32)).astype(jnp.bfloat16)
    return high, low


def dot(a, b, dims):
    return lax.dot_general(a, b, (dims, ((), ())), preferred_element_type=F32)


def spectra_kernel(
    nf, rows, np_, nt, kern_hbm, foc_hbm, ons_ref, tab_ref, out_hbm,
    kern_v, foc_v, spec_f, spec_s, spec_r, acc, part_s, part_r, g_s, g_r, g_f, dk,
    m_s, m_r, m_o, acc2, h_s,
    load_sem, s1, r1, sp, rp, s2, r2, s3, r3, so, ro, s4, r4,
):
    me = lax.axis_index("freq")
    core = lax.axis_index("rcv")
    nk = 2 * nf
    half = nf * rows
    sub = rows // NSUB
    per = max(1, 128 // rows)
    chunk = per * rows
    nch = half // chunk

    def dest_of(d):
        return lax.rem(me - d + nf, nf)

    def src_of(d):
        return lax.rem(me + d, nf)

    def peer(src, dst, ssem, rsem, dest):
        return pltpu.make_async_remote_copy(
            src_ref=src, dst_ref=dst, send_sem=ssem, recv_sem=rsem,
            device_id={"freq": dest}, device_id_type=MESH)

    def mate(src, dst, ssem, rsem):
        return pltpu.make_async_remote_copy(
            src_ref=src, dst_ref=dst, send_sem=ssem, recv_sem=rsem,
            device_id={"rcv": 1 - core}, device_id_type=MESH)

    def c1(d, b):
        w = pl.ds(b * sub, sub)
        return peer(spec_s.at[dest_of(d), :, w], spec_r.at[me, :, w], s1.at[b, d], r1.at[b, d], dest_of(d))

    def cp(d):
        return mate(part_s.at[d], part_r.at[d], sp.at[d], rp.at[d])

    def c2(d):
        return peer(g_s.at[dest_of(d)], g_r.at[me], s2.at[d], r2.at[d], dest_of(d))

    def c3(d):
        return peer(m_s.at[dest_of(d)], m_r.at[me], s3.at[d], r3.at[d], dest_of(d))

    def co(d):
        return mate(m_r.at[src_of(d)], m_o.at[src_of(d)], so.at[d], ro.at[d])

    def c4(d):
        return peer(h_s.at[dest_of(d)], out_hbm.at[me], s4.at[d], r4.at[d], dest_of(d))

    loads = [pltpu.make_async_copy(foc_hbm.at[pl.ds(b * sub, sub)], foc_v.at[pl.ds(b * sub, sub)], load_sem.at[b])
             for b in range(NSUB)]
    kload = pltpu.make_async_copy(kern_hbm.at[0], kern_v, load_sem.at[NSUB])
    for load in loads:
        load.start()
    kload.start()

    barrier = pltpu.get_barrier_semaphore()

    @pl.loop(1, nf)
    def _(d):
        pl.semaphore_signal(barrier, inc=1, device_id={"freq": dest_of(d)}, device_id_type=MESH)

    pl.semaphore_signal(barrier, inc=1, device_id={"rcv": 1 - core}, device_id_type=MESH)

    for b in range(NSUB):
        loads[b].wait()

        @pl.loop(0, sub // 2, unroll=4)
        def _(i):
            x = b * sub + 2 * i
            f = foc_v[pl.ds(x, 2)].reshape(2 * np_, nt)
            s = dot(tab_ref[...], f, ((1,), (1,)))
            s = s[:nk] + s[nk:]
            spec_f[pl.ds(x * nk, nk), :] = s[:, :np_]
            spec_f[pl.ds((x + 1) * nk, nk), :] = s[:, np_:]

        for k in range(nk):
            v = spec_f[pl.ds(b * sub * nk + k, sub, stride=nk), :]
            spec_s[k // 2, k % 2, pl.ds(b * sub, sub), :] = v.astype(BF)
        if b == 0:
            pl.semaphore_wait(barrier, nf)

        @pl.loop(1, nf)
        def _(d):
            c1(d, b).start()

    spec_r[me] = spec_s[me]

    theta = (ons_ref[...].astype(F32) - 0.5) * (2.0 * math.pi / nt)
    c_1, s_1 = jnp.cos(theta), jnp.sin(theta)
    dk[nf - 1] = (2.0 * ons_ref[...].astype(F32) - 1.0) * (1.0 / nt)
    cm, sm = c_1, s_1
    for m in range(1, 2 * nf + 1):
        value = sm * (1.0 / (nt * math.sin(math.pi * m / nt)))
        dk[nf - 1 + m] = value
        if m < nf:
            dk[nf - 1 - m] = value
        cm, sm = cm * c_1 - sm * s_1, sm * c_1 + cm * s_1

    acc[...] = jnp.zeros_like(acc)
    kload.wait()

    q0 = me // per

    def get_rhs(step):
        q = lax.rem(q0 + step, nch)

        @pl.loop(0, per)
        def _(j):
            d = lax.rem(q * per + j - me + nf, nf)

            @pl.when(d != 0)
            def _():
                for b in range(NSUB):
                    c1(d, b).wait_recv()

        s = spec_r[pl.ds(q * per, per)]
        re = s[:, 0].reshape(chunk, np_)
        im = s[:, 1].reshape(chunk, np_)
        rhs = jnp.concatenate(
            [jnp.concatenate([re, im], 1), jnp.concatenate([-im, re], 1)], 0)
        return pl.multiple_of(q * chunk, chunk), rhs

    tile = min(512, half)

    @pl.loop(0, nch - 1)
    def _(step):
        j, rhs = get_rhs(step)

        @pl.loop(0, 2 * half // tile)
        def _(t):
            w = pl.ds(pl.multiple_of(t * tile, tile), tile)
            lhs = jnp.concatenate([kern_v[0, w, pl.ds(j, chunk)], kern_v[1, w, pl.ds(j, chunk)]], 1)
            acc[w, :] += dot(lhs, rhs, ((1,), (0,)))

    j_last, rhs_last = get_rhs(nch - 1)

    def last(row):
        w = pl.ds(pl.multiple_of(row, rows), rows)
        lhs = jnp.concatenate([kern_v[0, w, pl.ds(j_last, chunk)], kern_v[1, w, pl.ds(j_last, chunk)]], 1)
        return acc[w, :] + dot(lhs, rhs_last, ((1,), (0,)))

    @pl.loop(1, nf + 1)
    def _(e):
        d = lax.rem(e, nf)
        part_s[d] = last((1 - core) * half + dest_of(d) * rows).astype(BF)
        cp(d).start()

    @pl.loop(1, nf + 1)
    def _(e):
        d = lax.rem(e, nf)
        own = last(core * half + dest_of(d) * rows)
        cp(d).wait_recv()
        g = (own + part_r[d].astype(F32)).astype(BF)
        g_s[dest_of(d), 0] = g[:, :np_]
        g_s[dest_of(d), 1] = g[:, np_:]

        @pl.when(d != 0)
        def _():
            c2(d).start()

    g_f[me] = g_s[me].astype(F32)

    @pl.loop(1, nf)
    def _(d):
        c2(d).wait_recv()
        g_f[src_of(d)] = g_r[src_of(d)].astype(F32)

    @pl.loop(1, nf + 1)
    def _(e):
        d = lax.rem(e, nf)
        a = dest_of(d)

        @pl.loop(0, rows // 16)
        def _(t):
            w = pl.ds(pl.multiple_of(t * 16, 16), 16)
            re = jnp.zeros((16, np_), F32)
            im = jnp.zeros((16, np_), F32)
            for f in range(nf):
                lo = dk[a - f + nf - 1, w, :]
                hi = dk[a + f + nf + 1, w, :]
                re = re + (lo + hi) * g_f[f, 0, w, :]
                im = im + (lo - hi) * g_f[f, 1, w, :]
            m_s[a, 0, w, :] = re.astype(BF)
            m_s[a, 1, w, :] = im.astype(BF)

        @pl.when(d != 0)
        def _():
            c3(d).start()

    m_r[me] = m_s[me]
    acc2[...] = jnp.zeros_like(acc2)

    def adjoint(buf, owner, src):
        mr, mi = buf[src, 0], buf[src, 1]
        lhs = jnp.concatenate(
            [jnp.concatenate([mr, mi], 1), jnp.concatenate([mi, -mr], 1)], 0)
        w = pl.ds(pl.multiple_of(owner * half + src * rows, rows), rows)
        rhs = jnp.concatenate([kern_v[0, w, :], kern_v[1, w, :]], 0)
        acc2[...] += dot(lhs, rhs, ((0,), (0,)))

    @pl.loop(0, nf)
    def _(d):
        @pl.when(d != 0)
        def _():
            c3(d).wait_recv()

        co(d).start()
        adjoint(m_r, core, src_of(d))

        @pl.when(d != 0)
        def _():
            co(d - 1).wait_recv()
            adjoint(m_o, 1 - core, src_of(d - 1))

    co(nf - 1).wait_recv()
    adjoint(m_o, 1 - core, src_of(nf - 1))

    @pl.loop(1, nch + 1)
    def _(e):
        q = lax.rem(q0 - e + 2 * nch, nch)
        w = pl.ds(pl.multiple_of(q * chunk, chunk), chunk)
        for c in range(2):
            t = jnp.swapaxes(acc2[pl.ds(c * np_, np_), w], 0, 1).astype(BF)
            h_s[pl.ds(q * per, per), c] = t.reshape(per, rows, np_)

        @pl.loop(0, per)
        def _(j):
            d = lax.rem(me - (q * per + j) + nf, nf)

            @pl.when(d != 0)
            def _():
                c4(d).start()

    keep = pltpu.make_async_copy(h_s.at[me], out_hbm.at[me], load_sem.at[0])
    keep.start()

    @pl.loop(1, nf)
    def _(d):
        c4(d).wait_recv()

    @pl.loop(1, nf)
    def _(d):
        for b in range(NSUB):
            c1(d, b).wait_send()
        c2(d).wait_send()
        c3(d).wait_send()
        c4(d).wait_send()

    @pl.loop(0, nf)
    def _(d):
        cp(d).wait_send()
        co(d).wait_send()

    keep.wait()


def final_kernel(nf, step_rows, np_, nt, h_ref, ons_ref, foc_ref, tab_ref, out_ref, rows_f):
    nk = 2 * nf
    width = nk + 16
    for k in range(nk):
        rows_f[pl.ds(k, step_rows, stride=width), :] = h_ref[k // 2, k % 2].astype(F32)
    rows_f[pl.ds(nk, step_rows, stride=width), :] = ons_ref[...].astype(F32)
    for k in range(nk + 1, width):
        rows_f[pl.ds(k, step_rows, stride=width), :] = jnp.full((step_rows, np_), 1.0 if k == nk + 1 else 0.0, F32)
    for x in range(step_rows):
        r = rows_f[pl.ds(x * width, width), :].astype(BF)
        lhs = jnp.concatenate([r[:nk], r], 0)
        both = dot(lhs, tab_ref[...], ((0,), (0,)))
        f = foc_ref[x].astype(F32)
        out_ref[x] = (f + jnp.where(both[:, nt:] > 0.0, both[:, :nt], 0.0)).astype(BF)


def shards(kernel, focus, onset):
    nf = lax.axis_size("freq")
    rows, np_, nt = focus.shape
    half = nf * rows
    start = (lax.axis_index("rcv") * nf + lax.axis_index("freq")) * rows
    own = lax.dynamic_slice_in_dim(onset, start, rows, 0)
    table = forward_table(nt, nf)
    fwd = jnp.asarray(np.concatenate(split(table), 0))
    inv_hi, inv_lo = split((table * np.float32(2.0 / nt)).astype(np.float32))
    nk = 2 * nf
    t = np.arange(nt)
    right = np.zeros((2 * nk + 16, 2 * nt), np.float32).astype(jnp.bfloat16)
    right[:nk, :nt] = inv_hi
    right[nk:2 * nk, :nt] = inv_lo
    right[2 * nk, nt:] = 1.0
    right[2 * nk + 1, nt:] = -np.minimum(t, nt - t)
    right = jnp.asarray(right)

    def vm(shape, kind=BF):
        return pltpu.VMEM(shape, kind)

    block = (nf, 2, rows, np_)
    dma = pltpu.SemaphoreType.DMA
    spectra = pl.pallas_call(
        functools.partial(spectra_kernel, nf, rows, np_, nt),
        out_shape=jax.ShapeDtypeStruct(block, BF),
        in_specs=[pl.BlockSpec(memory_space=pl.ANY)] * 2 + [pl.BlockSpec(memory_space=pltpu.VMEM)] * 2,
        out_specs=pl.BlockSpec(memory_space=pl.ANY),
        scratch_shapes=[
            vm((2, 2 * half, half)), vm((rows, np_, nt)), vm((rows * nk, np_), F32),
            vm(block), vm(block), vm((2 * half, 2 * np_), F32),
            vm((nf, rows, 2 * np_)), vm((nf, rows, 2 * np_)),
            vm(block), vm(block), vm(block, F32), vm((3 * nf, rows, np_), F32),
            vm(block), vm(block), vm(block), vm((2 * np_, half), F32), vm(block),
            dma((NSUB + 1,)), dma((NSUB, nf)), dma((NSUB, nf)),
        ] + [dma((nf,))] * 10,
        compiler_params=pltpu.CompilerParams(
            collective_id=0, has_side_effects=True, vmem_limit_bytes=56 << 20),
        cost_estimate=pl.CostEstimate(
            flops=32 * half * half * np_, bytes_accessed=8 * half * half, transcendentals=0),
    )(kernel, focus, own, fwd)
    sr = 16
    return pl.pallas_call(
        functools.partial(final_kernel, nf, sr, np_, nt),
        out_shape=jax.ShapeDtypeStruct(focus.shape, BF),
        grid=(rows // sr,),
        in_specs=[
            pl.BlockSpec((nf, 2, sr, np_), lambda i: (0, 0, i, 0)),
            pl.BlockSpec((sr, np_), lambda i: (i, 0)),
            pl.BlockSpec((sr, np_, nt), lambda i: (i, 0, 0)),
            pl.BlockSpec(right.shape, lambda i: (0, 0)),
        ],
        out_specs=pl.BlockSpec((sr, np_, nt), lambda i: (i, 0, 0)),
        scratch_shapes=[pltpu.VMEM((sr * (nk + 16), np_), F32)],
        compiler_params=pltpu.CompilerParams(vmem_limit_bytes=32 << 20),
    )(spectra, own, focus, right)


def solution(mesh):
    in_specs = (P("freq", None, None, "rcv"), P(("rcv", "freq"), "grp", None), P(None, "grp"))
    out_specs = P(("rcv", "freq"), "grp", None)
    return jax.shard_map(shards, mesh=mesh, in_specs=in_specs, out_specs=out_specs, check_vma=False)
```

time: 183 us -> 85.4 us (0.47)
  Pallas kernels: 0 us -> 78.4 us
  matrix products: 65.1 us -> 0 us
  blocking collectives: 60.2 us -> 0 us
  waiting for transfers between devices: 30.9 us -> 0 us
  between operations: 13.6 us -> 0.04 us
  starting transfers between devices: 5.99 us -> 0 us
  other arithmetic: 3.89 us -> 0 us
  local copies, waits for them, and re-layouts: 2.61 us -> 6.28 us
    pallas_call x0 -> x2, Pallas kernels: none -> 78.4 us  [the longest x1 69.8 us: shards(): pl.pallas_call(functools.partial(spectra_kernel, nf, rows, np_, nt), out_...]
    dot_general x12 -> x0, matrix products: 65.1 us -> none  [the longest x1 16.7 us: shards(): jnp.einsum('xpt,fct->fcxp', minus, forward, precision=highest)]
    all_to_all x3 -> x0, blocking collectives: 60.2 us -> none  [the longest x1 21.6 us: shards(): spec = lax.all_to_all(spec, 'freq', split_axis=0, concat_axis=2, tiled=True)]
    all_to_all x1 -> x0, waiting for transfers between devices: 13.9 us -> none  [shards(): lax.all_to_all(summed, 'freq', split_axis=2, concat_axis=0, tiled=True)]
    reduce_scatter x1 -> x0, waiting for transfers between devices: 8.76 us -> none  [shards(): lax.psum_scatter(partial_value, 'rcv', scatter_dimension=2, tiled=True)]
    all_gather x1 -> x0, waiting for transfers between devices: 8.24 us -> none  [shards(): returned = lax.all_gather(returned, 'rcv', axis=2, tiled=True)]
    all_to_all x1 -> x0, starting transfers between devices: 5.77 us -> none  [shards(): lax.all_to_all(summed, 'freq', split_axis=2, concat_axis=0, tiled=True)]
    unnamed x4 -> x10, local copies, waits for them, and re-layouts: 0.01 us -> 5.65 us
  transfers between devices with their start and end apart: 3 -> 0, of which waited for: 3 -> 0; matrix products, arithmetic and copies ran while one was open for 0% -> 0% of each run, Pallas kernels for 0% -> 0%
where the time goes in v1:
time: 85.4 us; the launch traced here: 84.7 us
  Pallas kernels  78.4 us (92%)
  local copies, waits for them, and re-layouts  6.28 us (7%)
    pallas_call x1, Pallas kernels, shards(): pl.pallas_call(functools.partial(spectra_kernel, nf, rows, np_, nt), out_...  69.8 us
    pallas_call x1, Pallas kernels, shards(): pl.pallas_call(functools.partial(final_kernel, nf, sr, np_, nt), out_shap...  8.53 us
    unnamed x10, local copies, waits for them, and re-layouts  5.65 us

profile of v1, /device:TPU:0, one launch (start us, length us, event | category | flops | bytes accessed | tf_op | source)
XLA Modules:
  0.0 84.7 jit_solution(5242603533836956755)
XLA Ops:
  0.0 0.0 copy-start
  0.0 1.2 %copy-done = s32[2048,128]{1,0:T(8,128)S(1)} copy-done((s32[2048,128]{1,0:T(8,128)S(1)}, s32[2048,128]{1,0:T(8,128)}, u32[]{:S(2)}) %copy-start) | copy-done | bytes 1048600
  1.2 0.6 constant_dynamic-slice_fusion.ons_ref
  1.9 0.0 copy-start.3
  1.9 0.0 copy-start.4
  1.9 69.8 %shard_map.55.h_ref = bf16[8,2,128,128]{3,2,1,0:T(8,128)(2,1)} custom-call(bf16[1,2,2048,1024]{3,2,1,0:T(8,128)(2,1)} %kern_hbm.1, bf16[128,128,256]{2,1,0:T(8,128)(2,1)} %foc_ref.1, s32[128,128]{1,0:T(8,128)} %constant_dynamic-slice_fusion.ons_ref, bf16[32,256]{1,0:T(8,128)(2,1)} %constant.20.clone.tab_ref), custom_call_target="tpu_custom_call" | custom-call | flops 4294967296 | bytes 8388608 | tf_op jit(solution)/shard_map/pallas_call | solution.py:330
  71.7 0.0 copy-done.3
  71.7 0.0 copy-done.4
  71.7 0.0 copy-start.1
  71.7 3.4 %copy-done.1 = bf16[128,128,256]{2,1,0:T(8,128)(2,1)S(1)} copy-done((bf16[128,128,256]{2,1,0:T(8,128)(2,1)S(1)}, bf16[128,128,256]{2,1,0:T(8,128)(2,1)}, u32[]{:S(2)}) %copy-start.1) | copy-done | bytes 8388632
  75.1 0.0 copy-start.2
  75.1 1.0 %copy-done.2 = bf16[8,2,128,128]{3,2,1,0:T(8,128)(2,1)S(1)} copy-done((bf16[8,2,128,128]{3,2,1,0:T(8,128)(2,1)S(1)}, bf16[8,2,128,128]{3,2,1,0:T(8,128)(2,1)}, u32[]{:S(2)}) %copy-start.2) | copy-done | bytes 524312
  76.2 8.5 %shard_map.56 = bf16[128,128,256]{2,1,0:T(8,128)(2,1)} custom-call(bf16[8,2,128,128]{3,2,1,0:T(8,128)(2,1)S(1)} %copy-done.2, s32[128,128]{1,0:T(8,128)S(1)} %copy-done.3, bf16[128,128,256]{2,1,0:T(8,128)(2,1)S(1)} %copy-done.1, bf16[48,512]{1,0:T(8,128)(2,1)S(1)} %copy-done.4), custom_call_target="tpu_custom_call" | custom-call | tf_op jit(solution)/shard_map/pallas_call | solution.py:349
Async XLA Ops:
  0.0 1.2 %copy-start = (s32[2048,128]{1,0:T(8,128)S(1)}, s32[2048,128]{1,0:T(8,128)}, u32[]{:S(2)}) copy-start(s32[2048,128]{1,0:T(8,128)} %param.7) | copy-start | bytes 3145732
  1.9 69.8 %copy-start.3 = (s32[128,128]{1,0:T(8,128)S(1)}, s32[128,128]{1,0:T(8,128)}, u32[]{:S(2)}) copy-start(s32[128,128]{1,0:T(8,128)} %constant_dynamic-slice_fusion.ons_ref) | copy-start | bytes 196612
  1.9 69.9 %copy-start.4 = (bf16[48,512]{1,0:T(8,128)(2,1)S(1)}, bf16[48,512]{1,0:T(8,128)(2,1)}, u32[]{:S(2)}) copy-start(bf16[48,512]{1,0:T(8,128)(2,1)} %constant.21.clone.tab_ref) | copy-start | bytes 147460
  71.7 3.4 %copy-start.1 = (bf16[128,128,256]{2,1,0:T(8,128)(2,1)S(1)}, bf16[128,128,256]{2,1,0:T(8,128)(2,1)}, u32[]{:S(2)}) copy-start(bf16[128,128,256]{2,1,0:T(8,128)(2,1)} %foc_ref.1) | copy-start | bytes 25165828
  75.1 1.0 %copy-start.2 = (bf16[8,2,128,128]{3,2,1,0:T(8,128)(2,1)S(1)}, bf16[8,2,128,128]{3,2,1,0:T(8,128)(2,1)}, u32[]{:S(2)}) copy-start(bf16[8,2,128,128]{3,2,1,0:T(8,128)(2,1)} %shard_map.55.h_ref) | copy-start | bytes 1572868

commit v2 on v0

v2 whole, which is shorter than its diff:
```python
import functools
import math

import jax
import jax.numpy as jnp
import numpy as np
from jax import lax
from jax.experimental import pallas as pl
from jax.experimental.pallas import tpu as pltpu
from jax.sharding import PartitionSpec as P

MESH = pl.DeviceIdType.MESH
NSUB = 2
BF = jnp.bfloat16
F32 = jnp.float32


def forward_table(nt, nf):
    phase = ((np.arange(1, nf + 1)[:, None] * np.arange(nt)[None, :]) % nt) * (2.0 * math.pi / nt)
    return np.stack([np.cos(phase), -np.sin(phase)], axis=1).reshape(2 * nf, nt).astype(np.float32)


def split(table):
    high = table.astype(jnp.bfloat16)
    low = (table - high.astype(np.float32)).astype(jnp.bfloat16)
    return high, low


def dot(a, b, dims):
    return lax.dot_general(a, b, (dims, ((), ())), preferred_element_type=F32)


def swap(block, first):
    h = block.shape[1] // 2
    re, im = block[:, :h], block[:, h:]
    return jnp.concatenate([-im, re] if first else [im, -re], 1)


def spectra_kernel(
    nf, rows, np_, nt, kern_hbm, foc_hbm, ons_hbm, tab_ref, out_hbm, ons_out,
    kern_v, foc_v, ons_v, spec_f, spec_s, spec_r, acc, part_s, part_r, g_s, g_r, g_f, dk,
    m_s, m_r, m_o, acc2, h_s,
    load_sem, s1, r1, sp, rp, s2, r2, s3, r3, so, ro, s4, r4,
):
    me = lax.axis_index("freq")
    core = lax.axis_index("rcv")
    nk = 2 * nf
    ph = np_ // 2
    half = nf * rows
    sub = rows // NSUB
    per = max(1, 128 // rows)
    chunk = per * rows
    nch = half // chunk
    nd = 2 * nf - 1

    def dest_of(d):
        return lax.rem(me - d + nf, nf)

    def src_of(d):
        return lax.rem(me + d, nf)

    def peer(src, dst, ssem, rsem, dest):
        return pltpu.make_async_remote_copy(
            src_ref=src, dst_ref=dst, send_sem=ssem, recv_sem=rsem,
            device_id={"freq": dest}, device_id_type=MESH)

    def mate(src, dst, ssem, rsem):
        return pltpu.make_async_remote_copy(
            src_ref=src, dst_ref=dst, send_sem=ssem, recv_sem=rsem,
            device_id={"rcv": 1 - core}, device_id_type=MESH)

    def c1(d, h, b):
        w = pl.ds(b * sub, sub) if h == 0 else pl.ds(0, rows)
        i = b if h == 0 else NSUB
        return peer(spec_s.at[h, dest_of(d), w], spec_r.at[h, me, w], s1.at[i, d], r1.at[i, d], dest_of(d))

    def cp(d, h):
        return mate(part_s.at[h, d], part_r.at[h, d], sp.at[h, d], rp.at[h, d])

    def c2(d, h):
        return peer(g_s.at[h, dest_of(d)], g_r.at[h, me], s2.at[h, d], r2.at[h, d], dest_of(d))

    def c3(d, h):
        return peer(m_s.at[h, dest_of(d)], m_r.at[h, me], s3.at[h, d], r3.at[h, d], dest_of(d))

    def co(d, h):
        return mate(m_r.at[h, src_of(d)], m_o.at[h, src_of(d)], so.at[h, d], ro.at[h, d])

    def c4(d, h):
        return peer(h_s.at[h, dest_of(d)], out_hbm.at[h, me], s4.at[h, d], r4.at[h, d], dest_of(d))

    loads = [pltpu.make_async_copy(foc_hbm.at[pl.ds(b * sub, sub)], foc_v.at[pl.ds(b * sub, sub)], load_sem.at[b])
             for b in range(NSUB)]
    kload = pltpu.make_async_copy(kern_hbm.at[0], kern_v, load_sem.at[NSUB])
    oload = pltpu.make_async_copy(
        ons_hbm.at[pl.ds(pl.multiple_of((core * nf + me) * rows, rows), rows)], ons_v, load_sem.at[NSUB + 1])
    for load in loads:
        load.start()
    oload.start()
    kload.start()

    barrier = pltpu.get_barrier_semaphore()

    @pl.loop(1, nf)
    def _(d):
        pl.semaphore_signal(barrier, inc=1, device_id={"freq": dest_of(d)}, device_id_type=MESH)

    pl.semaphore_signal(barrier, inc=1, device_id={"rcv": 1 - core}, device_id_type=MESH)

    for b in range(NSUB):
        loads[b].wait()

        @pl.loop(0, sub // 2, unroll=4)
        def _(i):
            x = b * sub + 2 * i
            f = foc_v[pl.ds(x, 2)].reshape(2 * np_, nt)
            s = dot(tab_ref[...], f, ((1,), (1,)))
            s = s[:nk] + s[nk:]
            for y in range(2):
                for h in range(2):
                    lo = y * np_ + h * ph
                    spec_f[h, pl.ds((x + y) * nf, nf), :] = jnp.concatenate(
                        [s[:nf, lo:lo + ph], s[nf:, lo:lo + ph]], 1)

        for h in range(2):
            for k in range(nf):
                v = spec_f[h, pl.ds(b * sub * nf + k, sub, stride=nf), :]
                spec_s[h, k, pl.ds(b * sub, sub), :] = v.astype(BF)
            if h == 0:
                if b == 0:
                    pl.semaphore_wait(barrier, nf)

                @pl.loop(1, nf)
                def _(d):
                    c1(d, 0, b).start()

    @pl.loop(1, nf)
    def _(d):
        c1(d, 1, 0).start()

    for h in range(2):
        spec_r[h, me] = spec_s[h, me]

    oload.wait()
    okeep = pltpu.make_async_copy(ons_v, ons_out, load_sem.at[NSUB + 1])
    okeep.start()
    real = lax.broadcasted_iota(jnp.int32, (rows, np_), 1) < ph
    for h in range(2):
        on = ons_v[:, h * ph:(h + 1) * ph].astype(F32)
        on = jnp.concatenate([on, on], 1)
        theta = (on - 0.5) * (2.0 * math.pi / nt)
        c_1, s_1 = jnp.cos(theta), jnp.sin(theta)
        dk[h, nf - 1] = (2.0 * on - 1.0) * (1.0 / nt)
        cm, sm = c_1, s_1
        for m in range(1, 2 * nf + 1):
            value = sm * (1.0 / (nt * math.sin(math.pi * m / nt)))
            if m < nf:
                dk[h, nf - 1 + m] = value
                dk[h, nf - 1 - m] = value
            if m > 1:
                dk[h, nd + m - 2] = jnp.where(real, value, -value)
            cm, sm = cm * c_1 - sm * s_1, sm * c_1 + cm * s_1

    acc[...] = jnp.zeros_like(acc)
    acc2[...] = jnp.zeros_like(acc2)
    kload.wait()

    q0 = me // per
    tile = min(512, half)

    def forward_product(h):
        def get_rhs(step):
            q = lax.rem(q0 + step, nch)

            @pl.loop(0, per)
            def _(j):
                d = lax.rem(q * per + j - me + nf, nf)

                @pl.when(d != 0)
                def _():
                    for b in range(NSUB if h == 0 else 1):
                        c1(d, h, b).wait_recv()

            s = spec_r[h, pl.ds(q * per, per)].reshape(chunk, np_)
            return pl.multiple_of(q * chunk, chunk), jnp.concatenate([s, swap(s, True)], 0)

        @pl.loop(0, nch - 1)
        def _(step):
            j, rhs = get_rhs(step)

            @pl.loop(0, 2 * half // tile)
            def _(t):
                w = pl.ds(pl.multiple_of(t * tile, tile), tile)
                lhs = jnp.concatenate([kern_v[0, w, pl.ds(j, chunk)], kern_v[1, w, pl.ds(j, chunk)]], 1)
                acc[h, w, :] += dot(lhs, rhs, ((1,), (0,)))

        j_last, rhs_last = get_rhs(nch - 1)

        def last(row):
            w = pl.ds(pl.multiple_of(row, rows), rows)
            lhs = jnp.concatenate(
                [kern_v[0, w, pl.ds(j_last, chunk)], kern_v[1, w, pl.ds(j_last, chunk)]], 1)
            return acc[h, w, :] + dot(lhs, rhs_last, ((1,), (0,)))

        @pl.loop(1, nf + 1)
        def _(e):
            d = lax.rem(e, nf)
            part_s[h, d] = last((1 - core) * half + dest_of(d) * rows).astype(BF)
            cp(d, h).start()

        @pl.loop(1, nf + 1)
        def _(e):
            d = lax.rem(e, nf)
            own = last(core * half + dest_of(d) * rows)
            cp(d, h).wait_recv()
            g_s[h, dest_of(d)] = (own + part_r[h, d].astype(F32)).astype(BF)

            @pl.when(d != 0)
            def _():
                c2(d, h).start()

    def window(h):
        g_f[me] = g_s[h, me].astype(F32)

        @pl.loop(1, nf)
        def _(d):
            c2(d, h).wait_recv()
            g_f[src_of(d)] = g_r[h, src_of(d)].astype(F32)

        @pl.loop(1, nf + 1)
        def _(e):
            d = lax.rem(e, nf)
            a = dest_of(d)

            @pl.loop(0, rows // 16)
            def _(t):
                w = pl.ds(pl.multiple_of(t * 16, 16), 16)
                total = jnp.zeros((16, np_), F32)
                for f in range(nf):
                    total = total + (dk[h, a - f + nf - 1, w, :] + dk[h, a + f + nd, w, :]) * g_f[f, w, :]
                m_s[h, a, w, :] = total.astype(BF)

            @pl.when(d != 0)
            def _():
                c3(d, h).start()

        m_r[h, me] = m_s[h, me]

    def adjoint_product(h):
        def add(buf, owner, src):
            m = buf[h, src]
            lhs = jnp.concatenate([m, swap(m, False)], 0)
            w = pl.ds(pl.multiple_of(owner * half + src * rows, rows), rows)
            rhs = jnp.concatenate([kern_v[0, w, :], kern_v[1, w, :]], 0)
            acc2[h] += dot(lhs, rhs, ((0,), (0,)))

        @pl.loop(0, nf)
        def _(d):
            @pl.when(d != 0)
            def _():
                c3(d, h).wait_recv()

            co(d, h).start()
            add(m_r, core, src_of(d))

            @pl.when(d != 0)
            def _():
                co(d - 1, h).wait_recv()
                add(m_o, 1 - core, src_of(d - 1))

        co(nf - 1, h).wait_recv()
        add(m_o, 1 - core, src_of(nf - 1))

        @pl.loop(1, nch + 1)
        def _(e):
            q = lax.rem(q0 - e + 2 * nch, nch)
            w = pl.ds(pl.multiple_of(q * chunk, chunk), chunk)
            t = jnp.swapaxes(acc2[h, :, w], 0, 1).astype(BF)
            h_s[h, pl.ds(q * per, per)] = t.reshape(per, rows, np_)

            @pl.loop(0, per)
            def _(j):
                d = lax.rem(me - (q * per + j) + nf, nf)

                @pl.when(d != 0)
                def _():
                    c4(d, h).start()

    for stage in (forward_product, window, adjoint_product):
        for h in range(2):
            stage(h)

    keep = [pltpu.make_async_copy(h_s.at[h, me], out_hbm.at[h, me], load_sem.at[h]) for h in range(2)]
    for h in range(2):
        keep[h].start()

    @pl.loop(1, nf)
    def _(d):
        for b in range(NSUB):
            c1(d, 0, b).wait_send()
        c1(d, 1, 0).wait_send()
        for h in range(2):
            c2(d, h).wait_send()
            c3(d, h).wait_send()
            c4(d, h).wait_send()

    @pl.loop(0, nf)
    def _(d):
        for h in range(2):
            cp(d, h).wait_send()
            co(d, h).wait_send()

    @pl.loop(1, nf)
    def _(d):
        for h in range(2):
            c4(d, h).wait_recv()

    okeep.wait()
    for h in range(2):
        keep[h].wait()


def final_kernel(nf, step_rows, width, np_, nt, h_ref, ons_ref, foc_ref, tab_ref, out_ref, rows_f):
    nk = 2 * nf
    ph = np_ // 2
    tied = 128 // width
    for f in range(nf):
        a, b = h_ref[0, f].astype(F32), h_ref[1, f].astype(F32)
        rows_f[pl.ds(f, step_rows, stride=width), :] = jnp.concatenate([a[:, :ph], b[:, :ph]], 1)
        rows_f[pl.ds(nf + f, step_rows, stride=width), :] = jnp.concatenate([a[:, ph:], b[:, ph:]], 1)
    rows_f[pl.ds(nk, step_rows, stride=width), :] = ons_ref[...].astype(F32)

    @pl.when(pl.program_id(0) == 0)
    def _():
        for k in range(nk + 1, width):
            rows_f[pl.ds(k, step_rows, stride=width), :] = jnp.full(
                (step_rows, np_), 1.0 if k == nk + 1 else 0.0, F32)

    groups = step_rows // tied
    cols = []
    for g in range(groups):
        t = jnp.swapaxes(rows_f[pl.ds(g * 128, 128), :], 0, 1).astype(BF)
        cols.append(jnp.concatenate([t, t], 1))
    for i in range(tied):
        for g in range(groups):
            x = g * tied + i
            both = dot(cols[g], tab_ref[i], ((1,), (0,)))
            f = foc_ref[x].astype(F32)
            out_ref[x] = (f + jnp.where(both[:, nt:] > 0.0, both[:, :nt], 0.0)).astype(BF)


def shards(kernel, focus, onset):
    nf = lax.axis_size("freq")
    rows, np_, nt = focus.shape
    half = nf * rows
    table = forward_table(nt, nf)
    nk = 2 * nf
    table = table.reshape(nf, 2, nt).swapaxes(0, 1).reshape(nk, nt)
    fwd = jnp.asarray(np.concatenate(split(table), 0))
    inv_hi, inv_lo = split((table * np.float32(2.0 / nt)).astype(np.float32))
    t = np.arange(nt)
    width = 32
    while width < nk + 2:
        width *= 2
    tied = 128 // width
    right = np.zeros((tied, 256, 2 * nt), np.float32).astype(jnp.bfloat16)
    for i in range(tied):
        at = i * width
        right[i, at:at + nk, :nt] = inv_hi
        right[i, 128 + at:128 + at + nk, :nt] = inv_lo
        right[i, at + nk, nt:] = 1.0
        right[i, at + nk + 1, nt:] = -np.minimum(t, nt - t)
    right = jnp.asarray(right)

    def vm(shape, kind=BF):
        return pltpu.VMEM(shape, kind)

    one = (nf, rows, np_)
    block = (2,) + one
    dma = pltpu.SemaphoreType.DMA
    spectra, own = pl.pallas_call(
        functools.partial(spectra_kernel, nf, rows, np_, nt),
        out_shape=[jax.ShapeDtypeStruct(block, BF), jax.ShapeDtypeStruct((rows, np_), jnp.int32)],
        in_specs=[pl.BlockSpec(memory_space=pl.ANY)] * 3 + [pl.BlockSpec(memory_space=pltpu.VMEM)],
        out_specs=[pl.BlockSpec(memory_space=pl.ANY)] * 2,
        scratch_shapes=[
            vm((2, 2 * half, half)), vm((rows, np_, nt)), vm((rows, np_), jnp.int32),
            vm((2, rows * nf, np_), F32),
            vm(block), vm(block), vm((2, 2 * half, np_), F32),
            vm(block), vm(block),
            vm(block), vm(block), vm(one, F32), vm((2, 4 * nf - 2, rows, np_), F32),
            vm(block), vm(block), vm(block), vm((2, np_, half), F32), vm(block),
            dma((NSUB + 2,)), dma((NSUB + 1, nf)), dma((NSUB + 1, nf)),
        ] + [dma((2, nf))] * 10,
        compiler_params=pltpu.CompilerParams(
            collective_id=0, has_side_effects=True, vmem_limit_bytes=58 << 20),
        cost_estimate=pl.CostEstimate(
            flops=32 * half * half * np_, bytes_accessed=8 * half * half, transcendentals=0),
    )(kernel, focus, onset, fwd)
    sr = 16
    return pl.pallas_call(
        functools.partial(final_kernel, nf, sr, width, np_, nt),
        out_shape=jax.ShapeDtypeStruct(focus.shape, BF),
        grid=(rows // sr,),
        in_specs=[
            pl.BlockSpec((2, nf, sr, np_), lambda i: (0, 0, i, 0)),
            pl.BlockSpec((sr, np_), lambda i: (i, 0)),
            pl.BlockSpec((sr, np_, nt), lambda i: (i, 0, 0)),
            pl.BlockSpec(right.shape, lambda i: (0, 0, 0)),
        ],
        out_specs=pl.BlockSpec((sr, np_, nt), lambda i: (i, 0, 0)),
        scratch_shapes=[pltpu.VMEM((sr * width, np_), F32)],
        compiler_params=pltpu.CompilerParams(vmem_limit_bytes=58 << 20),
    )(spectra, own, focus, right)


def solution(mesh):
    in_specs = (P("freq", None, None, "rcv"), P(("rcv", "freq"), "grp", None), P(None, "grp"))
    out_specs = P(("rcv", "freq"), "grp", None)
    return jax.shard_map(shards, mesh=mesh, in_specs=in_specs, out_specs=out_specs, check_vma=False)
```

time: 183 us -> 82.1 us (0.45)
  Pallas kernels: 0 us -> 81.7 us
  matrix products: 65.1 us -> 0 us
  blocking collectives: 60.2 us -> 0 us
  waiting for transfers between devices: 30.9 us -> 0 us
  between operations: 13.6 us -> 0.01 us
  starting transfers between devices: 5.99 us -> 0 us
  other arithmetic: 3.89 us -> 0 us
  local copies, waits for them, and re-layouts: 2.61 us -> 0 us
    pallas_call x0 -> x2, Pallas kernels: none -> 81.7 us  [the longest x1 69 us: shards(): pl.pallas_call(functools.partial(spectra_kernel, nf, rows, np_, nt), out_...]
    dot_general x12 -> x0, matrix products: 65.1 us -> none  [the longest x1 16.7 us: shards(): jnp.einsum('xpt,fct->fcxp', minus, forward, precision=highest)]
    all_to_all x3 -> x0, blocking collectives: 60.2 us -> none  [the longest x1 21.6 us: shards(): spec = lax.all_to_all(spec, 'freq', split_axis=0, concat_axis=2, tiled=True)]
    all_to_all x1 -> x0, waiting for transfers between devices: 13.9 us -> none  [shards(): lax.all_to_all(summed, 'freq', split_axis=2, concat_axis=0, tiled=True)]
    reduce_scatter x1 -> x0, waiting for transfers between devices: 8.76 us -> none  [shards(): lax.psum_scatter(partial_value, 'rcv', scatter_dimension=2, tiled=True)]
    all_gather x1 -> x0, waiting for transfers between devices: 8.24 us -> none  [shards(): returned = lax.all_gather(returned, 'rcv', axis=2, tiled=True)]
    all_to_all x1 -> x0, starting transfers between devices: 5.77 us -> none  [shards(): lax.all_to_all(summed, 'freq', split_axis=2, concat_axis=0, tiled=True)]
  transfers between devices with their start and end apart: 3 -> 0, of which waited for: 3 -> 0; matrix products, arithmetic and copies ran while one was open for 0% -> 0% of each run, Pallas kernels for 0% -> 0%
where the time goes in v2:
time: 82.1 us; the launch traced here: 81.7 us
  Pallas kernels  81.7 us (100%)
    pallas_call x1, Pallas kernels, shards(): pl.pallas_call(functools.partial(spectra_kernel, nf, rows, np_, nt), out_...  69 us
    pallas_call x1, Pallas kernels, shards(): pl.pallas_call(functools.partial(final_kernel, nf, sr, width, np_, nt), o...  12.6 us

profile of v2, /device:TPU:0, one launch (start us, length us, event | category | flops | bytes accessed | tf_op | source)
XLA Modules:
  0.0 81.7 jit_solution(17012259750013318264)
XLA Ops:
  0.0 69.0 %shard_map.55 = (bf16[2,8,128,128]{3,2,1,0:T(8,128)(2,1)}, s32[128,128]{1,0:T(8,128)}) custom-call(bf16[1,2,2048,1024]{3,2,1,0:T(8,128)(2,1)} %kern_hbm.1, bf16[128,128,256]{2,1,0:T(8,128)(2,1)} %foc_ref.1, s32[2048,128]{1,0:T(8,128)} %ons_hbm.1, bf16[32,256]{1,0:T(8,128)(2,1)} %constant.4.clone.tab_ref), custom_call_target="tpu_custom_call" | custom-call | flops 4294967296 | bytes 8388608 | tf_op jit(solution)/shard_map/pallas_call | solution.py:381
  69.0 12.6 %shard_map.56 = bf16[128,128,256]{2,1,0:T(8,128)(2,1)} custom-call(bf16[2,8,128,128]{3,2,1,0:T(8,128)(2,1)} %get-tuple-element.7.h_ref, s32[128,128]{1,0:T(8,128)} %get-tuple-element.8.ons_ref, bf16[128,128,256]{2,1,0:T(8,128)(2,1)} %foc_ref.1, bf16[4,256,512]{2,1,0:T(8,128)(2,1)} %constant.5.clone.tab_ref), custom_call_target="tpu_custom_call" | custom-call | tf_op jit(solution)/shard_map/pallas_call | solution.py:401

commit v3 on v2

--- a/solution.py
+++ b/solution.py
@@ -166,7 +166,7 @@
     kload.wait()
 
     q0 = me // per
-    tile = min(512, half)
+    tile = half
 
     def forward_product(h):
         def get_rhs(step):
@@ -333,20 +333,20 @@
     @pl.when(pl.program_id(0) == 0)
     def _():
         for k in range(nk + 1, width):
-            rows_f[pl.ds(k, step_rows, stride=width), :] = jnp.full(
-                (step_rows, np_), 1.0 if k == nk + 1 else 0.0, F32)
+            rows_f[pl.ds(k, step_rows, stride=width), :] = jnp.zeros((step_rows, np_), F32)
 
     groups = step_rows // tied
-    cols = []
+    sample = lax.broadcasted_iota(jnp.int32, (np_, nt), 1)
+    edge = jnp.minimum(sample, nt - sample).astype(F32)
     for g in range(groups):
-        t = jnp.swapaxes(rows_f[pl.ds(g * 128, 128), :], 0, 1).astype(BF)
-        cols.append(jnp.concatenate([t, t], 1))
-    for i in range(tied):
-        for g in range(groups):
+        t = jnp.swapaxes(rows_f[pl.ds(g * 128, 128), :], 0, 1)
+        col = t.astype(BF)
+        for i in range(tied):
             x = g * tied + i
-            both = dot(cols[g], tab_ref[i], ((1,), (0,)))
+            update = dot(jnp.concatenate([col, col], 1), tab_ref[i], ((1,), (0,)))
+            limit = t[:, i * width + nk:i * width + nk + 1]
             f = foc_ref[x].astype(F32)
-            out_ref[x] = (f + jnp.where(both[:, nt:] > 0.0, both[:, :nt], 0.0)).astype(BF)
+            out_ref[x] = (f + jnp.where(edge < limit, update, 0.0)).astype(BF)
 
 
 def shards(kernel, focus, onset):
@@ -358,18 +358,15 @@
     table = table.reshape(nf, 2, nt).swapaxes(0, 1).reshape(nk, nt)
     fwd = jnp.asarray(np.concatenate(split(table), 0))
     inv_hi, inv_lo = split((table * np.float32(2.0 / nt)).astype(np.float32))
-    t = np.arange(nt)
     width = 32
     while width < nk + 2:
         width *= 2
     tied = 128 // width
-    right = np.zeros((tied, 256, 2 * nt), np.float32).astype(jnp.bfloat16)
+    right = np.zeros((tied, 256, nt), np.float32).astype(jnp.bfloat16)
     for i in range(tied):
         at = i * width
-        right[i, at:at + nk, :nt] = inv_hi
-        right[i, 128 + at:128 + at + nk, :nt] = inv_lo
-        right[i, at + nk, nt:] = 1.0
-        right[i, at + nk + 1, nt:] = -np.minimum(t, nt - t)
+        right[i, at:at + nk] = inv_hi
+        right[i, 128 + at:128 + at + nk] = inv_lo
     right = jnp.asarray(right)
 
     def vm(shape, kind=BF):
@@ -397,7 +394,7 @@
         cost_estimate=pl.CostEstimate(
             flops=32 * half * half * np_, bytes_accessed=8 * half * half, transcendentals=0),
     )(kernel, focus, onset, fwd)
-    sr = 16
+    sr = min(rows, 32)
     return pl.pallas_call(
         functools.partial(final_kernel, nf, sr, width, np_, nt),
         out_shape=jax.ShapeDtypeStruct(focus.shape, BF),

time: 82.1 us -> 76 us (0.926)
  Pallas kernels: 81.7 us -> 75.8 us
    pallas_call x1, Pallas kernels: 69 us -> 65.7 us  [shards(): pl.pallas_call(functools.partial(spectra_kernel, nf, rows, np_, nt), out_...]
    pallas_call x1, Pallas kernels: 12.6 us -> 10.1 us  [shards(): pl.pallas_call(functools.partial(final_kernel, nf, sr, width, np_, nt), o...]
where the time goes in v3:
time: 76 us; the launch traced here: 75.8 us
  Pallas kernels  75.8 us (100%)
    pallas_call x1, Pallas kernels, shards(): pl.pallas_call(functools.partial(spectra_kernel, nf, rows, np_, nt), out_...  65.7 us
    pallas_call x1, Pallas kernels, shards(): pl.pallas_call(functools.partial(final_kernel, nf, sr, width, np_, nt), o...  10.1 us

profile of v3, /device:TPU:0, one launch (start us, length us, event | category | flops | bytes accessed | tf_op | source)
XLA Modules:
  0.0 75.8 jit_solution(1884115051515254878)
XLA Ops:
  0.0 65.7 %shard_map.55 = (bf16[2,8,128,128]{3,2,1,0:T(8,128)(2,1)}, s32[128,128]{1,0:T(8,128)}) custom-call(bf16[1,2,2048,1024]{3,2,1,0:T(8,128)(2,1)} %kern_hbm.1, bf16[128,128,256]{2,1,0:T(8,128)(2,1)} %foc_ref.1, s32[2048,128]{1,0:T(8,128)} %ons_hbm.1, bf16[32,256]{1,0:T(8,128)(2,1)} %constant.4.clone.tab_ref), custom_call_target="tpu_custom_call" | custom-call | flops 4294967296 | bytes 8388608 | tf_op jit(solution)/shard_map/pallas_call | solution.py:378
  65.7 10.1 %shard_map.56 = bf16[128,128,256]{2,1,0:T(8,128)(2,1)} custom-call(bf16[2,8,128,128]{3,2,1,0:T(8,128)(2,1)} %get-tuple-element.7.h_ref, s32[128,128]{1,0:T(8,128)} %get-tuple-element.8.ons_ref, bf16[128,128,256]{2,1,0:T(8,128)(2,1)} %foc_ref.1, bf16[4,256,256]{2,1,0:T(8,128)(2,1)} %constant.5.clone.tab_ref), custom_call_target="tpu_custom_call" | custom-call | tf_op jit(solution)/shard_map/pallas_call | solution.py:398

commit v4 on v3

--- a/solution.py
+++ b/solution.py
@@ -196,24 +196,30 @@
 
         j_last, rhs_last = get_rhs(nch - 1)
 
-        def last(row):
-            w = pl.ds(pl.multiple_of(row, rows), rows)
+        def last(owner):
+            w = pl.ds(pl.multiple_of(owner * half, half), half)
             lhs = jnp.concatenate(
                 [kern_v[0, w, pl.ds(j_last, chunk)], kern_v[1, w, pl.ds(j_last, chunk)]], 1)
-            return acc[h, w, :] + dot(lhs, rhs_last, ((1,), (0,)))
+            acc[h, w, :] += dot(lhs, rhs_last, ((1,), (0,)))
+
+        def block(owner, d):
+            return acc[h, pl.ds(pl.multiple_of(owner * half + dest_of(d) * rows, rows), rows), :]
+
+        last(1 - core)
 
         @pl.loop(1, nf + 1)
         def _(e):
             d = lax.rem(e, nf)
-            part_s[h, d] = last((1 - core) * half + dest_of(d) * rows).astype(BF)
+            part_s[h, d] = block(1 - core, d).astype(BF)
             cp(d, h).start()
+
+        last(core)
 
         @pl.loop(1, nf + 1)
         def _(e):
             d = lax.rem(e, nf)
-            own = last(core * half + dest_of(d) * rows)
             cp(d, h).wait_recv()
-            g_s[h, dest_of(d)] = (own + part_r[h, d].astype(F32)).astype(BF)
+            g_s[h, dest_of(d)] = (block(core, d) + part_r[h, d].astype(F32)).astype(BF)
 
             @pl.when(d != 0)
             def _():
@@ -247,29 +253,27 @@
         m_r[h, me] = m_s[h, me]
 
     def adjoint_product(h):
-        def add(buf, owner, src):
-            m = buf[h, src]
-            lhs = jnp.concatenate([m, swap(m, False)], 0)
-            w = pl.ds(pl.multiple_of(owner * half + src * rows, rows), rows)
-            rhs = jnp.concatenate([kern_v[0, w, :], kern_v[1, w, :]], 0)
-            acc2[h] += dot(lhs, rhs, ((0,), (0,)))
-
-        @pl.loop(0, nf)
+        def add(*terms):
+            lhs, rhs = [], []
+            for buf, owner, src in terms:
+                m = buf[h, src]
+                w = pl.ds(pl.multiple_of(owner * half + src * rows, rows), rows)
+                lhs += [m, swap(m, False)]
+                rhs += [kern_v[0, w, :], kern_v[1, w, :]]
+            acc2[h] += dot(jnp.concatenate(lhs, 0), jnp.concatenate(rhs, 0), ((0,), (0,)))
+
+        co(0, h).start()
+        add((m_r, core, me))
+
+        @pl.loop(1, nf)
         def _(d):
-            @pl.when(d != 0)
-            def _():
-                c3(d, h).wait_recv()
-
+            c3(d, h).wait_recv()
             co(d, h).start()
-            add(m_r, core, src_of(d))
-
-            @pl.when(d != 0)
-            def _():
-                co(d - 1, h).wait_recv()
-                add(m_o, 1 - core, src_of(d - 1))
+            co(d - 1, h).wait_recv()
+            add((m_r, core, src_of(d)), (m_o, 1 - core, src_of(d - 1)))
 
         co(nf - 1, h).wait_recv()
-        add(m_o, 1 - core, src_of(nf - 1))
+        add((m_o, 1 - core, src_of(nf - 1)))
 
         @pl.loop(1, nch + 1)
         def _(e):

time: 76 us -> 73.1 us (0.962)
  Pallas kernels: 75.8 us -> 72.9 us
    pallas_call x1, Pallas kernels: 65.7 us -> 62.8 us  [shards(): pl.pallas_call(functools.partial(spectra_kernel, nf, rows, np_, nt), out_...]
where the time goes in v4:
time: 73.1 us; the launch traced here: 72.9 us
  Pallas kernels  72.9 us (100%)
    pallas_call x1, Pallas kernels, shards(): pl.pallas_call(functools.partial(spectra_kernel, nf, rows, np_, nt), out_...  62.8 us
    pallas_call x1, Pallas kernels, shards(): pl.pallas_call(functools.partial(final_kernel, nf, sr, width, np_, nt), o...  10.1 us

profile of v4, /device:TPU:0, one launch (start us, length us, event | category | flops | bytes accessed | tf_op | source)
XLA Modules:
  0.0 72.9 jit_solution(14272771902979604605)
XLA Ops:
  0.0 62.8 %shard_map.55 = (bf16[2,8,128,128]{3,2,1,0:T(8,128)(2,1)}, s32[128,128]{1,0:T(8,128)}) custom-call(bf16[1,2,2048,1024]{3,2,1,0:T(8,128)(2,1)} %kern_hbm.1, bf16[128,128,256]{2,1,0:T(8,128)(2,1)} %foc_ref.1, s32[2048,128]{1,0:T(8,128)} %ons_hbm.1, bf16[32,256]{1,0:T(8,128)(2,1)} %constant.4.clone.tab_ref), custom_call_target="tpu_custom_call" | custom-call | flops 4294967296 | bytes 8388608 | tf_op jit(solution)/shard_map/pallas_call | solution.py:382
  62.8 10.1 %shard_map.56 = bf16[128,128,256]{2,1,0:T(8,128)(2,1)} custom-call(bf16[2,8,128,128]{3,2,1,0:T(8,128)(2,1)} %get-tuple-element.7.h_ref, s32[128,128]{1,0:T(8,128)} %get-tuple-element.8.ons_ref, bf16[128,128,256]{2,1,0:T(8,128)(2,1)} %foc_ref.1, bf16[4,256,256]{2,1,0:T(8,128)(2,1)} %constant.5.clone.tab_ref), custom_call_target="tpu_custom_call" | custom-call | tf_op jit(solution)/shard_map/pallas_call | solution.py:402
